TPU v7x, 256 devices: a whole 4x4x8 slice. The times are simulated.
256 devices in a mesh: dp: 32 (over y_lo, z, core), seq: 8 (over x, y_hi).
Axes of the slice: x: 4, y: 4 (y_hi: 2, y_lo: 2; y = y_hi * 2 + y_lo), z: 8, core: 2. Of those that a mesh axis runs over, the one named last changes fastest.
Arguments:
- text_context: bfloat16 [32, 128, 4096], P('dp', None, 'seq'), may hold values from -6 to 6
- text_residual: bfloat16 [32, 128, 4096], P('dp'), may hold values from -6 to 6
- text_out_weight: bfloat16 [4096, 4096], P('seq'), may hold values from -0.09375 to 0.09375
- text_gain: float32 [4096], replicated, may hold values from 0.1 to 1.9
- prompt_length: int32 [32], P('dp'), may hold values from 16 to 128, as said below
- key_weight: bfloat16 [4096, 3072], P('dp', 'seq'), may hold values from -0.09375 to 0.09375
- value_weight: bfloat16 [4096, 3072], P('dp', 'seq'), may hold values from -0.09375 to 0.09375
- video_query: bfloat16 [32, 1024, 3072], P('dp', 'seq'), may hold values from -100 to 100
- video_key: bfloat16 [32, 1024, 3072], P('dp', 'seq'), may hold values from -5.05 to 5.05
- video_value: bfloat16 [32, 1024, 3072], P('dp', 'seq'), may hold values from -6 to 6
- out_cotangent: bfloat16 [32, 1024, 3072], P('dp', 'seq'), may hold values from -6 to 6
Outputs:
- attended: bfloat16 [32, 1024, 3072], P('dp', 'seq')
- query_grad: bfloat16 [32, 1024, 3072], P('dp', 'seq')
- key_grad: bfloat16 [32, 1024, 3072], P('dp', 'seq')
- value_grad: bfloat16 [32, 1024, 3072], P('dp', 'seq')
- key_weight_grad: float32 [4096, 3072], P('dp', 'seq')
- value_weight_grad: float32 [4096, 3072], P('dp', 'seq')
Inputs may be any that keep to these rules, and one draw needn't show every extreme that they name: `prompt_length`: prompt slots from a clip's length on are padding; some clip of every draw has 128.
All inputs are finite; a program needn't handle non-finite values.
Results may differ from a plain program's by a relative error of at most 0.034.
Values may be sent and summed in bfloat16 or wider, within the bound.
A program may use at most 128 MiB of HBM per device.

v0:
```python
import math

import jax
import jax.numpy as jnp
from jax import lax
from jax.experimental import pallas as pl
from jax.experimental.pallas import tpu as pltpu
from jax.sharding import PartitionSpec as P

MESH = pl.DeviceIdType.MESH
BF = jnp.bfloat16
F32 = jnp.float32

HEAD_DIM = 128
EPSILON = 1e-06
SEQ = 8
ZS = 8
GROUP = 4
HEADS_HERE = 3
ROWS = 128
TOKENS = SEQ * ROWS
PROMPT = 128
ALL_ROWS = TOKENS + PROMPT
D_TEXT = 4096
SHARE = D_TEXT // SEQ
WIDTH = HEADS_HERE * HEAD_DIM
QUERY_BLOCK = 512
EXP2_SCALE = math.log2(math.e) / math.sqrt(HEAD_DIM)
SCALE = 1.0 / math.sqrt(HEAD_DIM)


def nn(left, right):
    return jnp.dot(left, right, preferred_element_type=F32)


def nt(left, right):
    return lax.dot_general(left, right, (((1,), (1,)), ((), ())), preferred_element_type=F32)


def tn(left, right):
    return lax.dot_general(left, right, (((0,), (0,)), ((), ())), preferred_element_type=F32)


def block128(index):
    return pl.ds(pl.multiple_of(index * 128, 128), 128)


def kernel(
    length_ref,
    context,
    gain,
    residual,
    out_weight,
    key_weight,
    value_weight,
    video_query,
    video_key,
    video_value,
    out_cotangent,
    attended,
    query_grad,
    key_grad,
    value_grad,
    key_weight_grad,
    value_weight_grad,
    q,
    k,
    v,
    do,
    out,
    dq,
    dk,
    dv,
    dk_total,
    dv_total,
    w_out,
    res,
    summed,
    part,
    part_in,
    piece,
    landed,
    text,
    text_t,
    wkv,
    kv_own,
    kv_core,
    kv_core_in,
    kv_far,
    kv_far_in,
    dkv_all,
    grads,
    grads_in,
    in_s,
    in_r,
    out_s,
    out_r,
    w_s,
    w_r,
    rs_s,
    rs_r,
    load_sem,
    res_sem,
    ag_s,
    ag_r,
    kc_s,
    kc_r,
    kf_s,
    kf_r,
    dk_s,
    dk_r,
    wg_s,
    wg_r,
):
    dp = lax.axis_index("dp")
    seq = lax.axis_index("seq")
    y_lo = dp // 16
    z = (dp // 2) % 8
    core = dp % 2

    def seq_of(d):
        return ((seq // 2 + d // 2) % 4) * 2 + (seq % 2 + d % 2) % 2

    def seq_peer(d):
        return (dp, seq_of(d))

    def group_peer(i, d):
        return (((y_lo + i // 2) % 2) * 16 + z * 2 + (core + i % 2) % 2, seq_of(d))

    def core_peer():
        return (dp + 1 - 2 * core, seq)

    def far_peer():
        return ((1 - y_lo) * 16 + z * 2 + core, seq)

    def z_peer(i):
        return (y_lo * 16 + ((z + i) % 8) * 2 + core, seq)

    def remote(src, dst, send, recv, peer):
        return pltpu.make_async_remote_copy(
            src_ref=src, dst_ref=dst, send_sem=send, recv_sem=recv, device_id=peer, device_id_type=MESH
        )

    def loop(low, high, step):
        def run(i, carry):
            step(i)
            return carry

        lax.fori_loop(low, high, run, 0)


    def w_load(d, half):
        columns = pl.ds(pl.multiple_of(half * 2048 + seq_of(d) * 256, 256), 256)
        return pltpu.make_async_copy(
            out_weight.at[:, columns], w_out.at[d, :, pl.ds(half * 256, 256)], load_sem.at[d, half]
        )

    def res_load(half):
        columns = pl.ds(pl.multiple_of(half * 2048 + seq * 256, 256), 256)
        return pltpu.make_async_copy(
            residual.at[:, columns], res.at[:, pl.ds(half * 256, 256)], res_sem.at[half]
        )

    def weight_copy(n, h, i):
        return remote(
            (key_weight, value_weight)[n].at[:, block128(h)],
            wkv.at[h, z, :, pl.ds(n * 128, 128)],
            w_s.at[n, h, i],
            w_r.at[n, h, i],
            z_peer(i),
        )

    def weight_own(n, h):
        return pltpu.make_async_copy(
            (key_weight, value_weight)[n].at[:, block128(h)],
            wkv.at[h, z, :, pl.ds(n * 128, 128)],
            w_r.at[n, h, 0],
        )

    sources = (video_query, video_key, video_value, out_cotangent)
    landings = (q, k, v, do)
    results = (out, dq, dk, dv)
    targets = (attended, query_grad, key_grad, value_grad)

    def in_copy(n, h, d):
        peer = seq_peer(d)
        return remote(
            sources[n].at[:, block128(peer[1] * HEADS_HERE + h)],
            landings[n].at[h, block128(seq)],
            in_s.at[n, h, d],
            in_r.at[n, h, d],
            peer,
        )

    def in_own(n, h):
        return pltpu.make_async_copy(
            sources[n].at[:, block128(seq * HEADS_HERE + h)],
            landings[n].at[h, block128(seq)],
            in_r.at[n, h, 0],
        )

    def out_copy(n, h, d):
        peer = seq_peer(d)
        return remote(
            results[n].at[h, block128(peer[1])],
            targets[n].at[:, block128(seq * HEADS_HERE + h)],
            out_s.at[n, h, d],
            out_r.at[n, h, d],
            peer,
        )

    def out_own(n, h):
        return pltpu.make_async_copy(
            results[n].at[h, block128(seq)],
            targets[n].at[:, block128(seq * HEADS_HERE + h)],
            out_r.at[n, h, 0],
        )

    def part_copy(d):
        return remote(part.at[d], part_in.at[d], rs_s.at[d], rs_r.at[d], seq_peer(d))

    def piece_copy(i, d):
        target = ((y_lo + i // 2) % 2) * 2 + (core + i % 2) % 2
        return remote(
            piece.at[target],
            landed.at[seq, (i % 2) * 2 + y_lo],
            ag_s.at[i, d],
            ag_r.at[i, d],
            group_peer(i, d),
        )

    def kv_core_copy(h):
        return remote(kv_core.at[h], kv_core_in.at[h], kc_s.at[h], kc_r.at[h], core_peer())

    def kv_far_copy(h):
        return remote(kv_far.at[h], kv_far_in.at[h], kf_s.at[h], kf_r.at[h], far_peer())

    def dkv_far(h):
        mine = dkv_all.at[h, y_lo]
        return remote(mine, mine, dk_s.at[h, 0], dk_r.at[h, 0], far_peer())

    def dkv_core(h, other):
        side = (1 - y_lo) if other else y_lo
        return remote(
            dkv_all.at[h, side],
            dkv_all.at[h, 2 + side],
            dk_s.at[h, 1 + other],
            dk_r.at[h, 1 + other],
            core_peer(),
        )

    def grad_copy(h, i):
        return remote(grads.at[h, (z + i) % 8], grads_in.at[h, i], wg_s.at[h, i], wg_r.at[h, i], z_peer(i))

    def send_head_in(h):
        for n in range(4):
            loop(1, SEQ, lambda d: in_copy(n, h, d).start())

    def all_group(step):
        loop(1, SEQ, lambda d: step(0, d))
        loop(1, GROUP, lambda i: loop(0, SEQ, lambda d: step(i, d)))


    barrier = pltpu.get_barrier_semaphore()

    def greet(peer):
        pl.semaphore_signal(barrier, inc=1, device_id=peer, device_id_type=MESH)

    all_group(lambda i, d: greet(group_peer(i, d)))
    loop(1, ZS, lambda i: greet(z_peer(i)))

    def start_loads(d):
        for half in range(2):
            w_load(d, half).start()

    loop(0, SEQ, start_loads)
    for half in range(2):
        res_load(half).start()
    for h in range(HEADS_HERE):
        for n in range(2):
            weight_own(n, h).start()
        for n in range(4):
            in_own(n, h).start()


    def project(d):
        for half in range(2):
            w_load(d, half).wait()
        return nn(context[...], w_out[d])

    for half in range(2):
        res_load(half).wait()
    summed[...] = project(0) + res[...].astype(F32)

    def project_step(d):
        part[d] = project(d).astype(BF)

    loop(1, SEQ, project_step)
    pl.semaphore_wait(barrier, GROUP * SEQ - 1 + ZS - 1)
    loop(1, SEQ, lambda d: part_copy(d).start())

    def send_weights(h):
        for n in range(2):
            loop(1, ZS, lambda i: weight_copy(n, h, i).start())

    send_weights(0)
    send_head_in(0)
    send_weights(1)
    send_weights(2)

    for d in range(1, SEQ):
        part_copy(d).wait_recv()
        summed[...] += part_in[d].astype(F32)
    total = summed[...]
    square = lax.dot_general(
        jnp.ones((16, SHARE), F32),
        total * total,
        (((1,), (1,)), ((), ())),
        precision=lax.Precision.HIGHEST,
        preferred_element_type=F32,
    )
    high = square.astype(BF).astype(F32)
    middle = (square - high).astype(BF).astype(F32)
    low = square - high - middle
    row = lax.broadcasted_iota(jnp.int32, (16, PROMPT), 0)
    square_rows = jnp.where(
        row == 0, high, jnp.where(row == 1, middle, jnp.where(row == 2, low, 0.0))
    ).astype(BF)
    for half in range(2):
        columns = pl.ds(pl.multiple_of(half * 2048 + seq * 256, 256), 256)
        scaled = (total[:, half * 256 : (half + 1) * 256] * gain[:, columns]).astype(BF)
        for c in range(2):
            piece[half * 2 + c, :PROMPT, :] = scaled[:, c * 128 : (c + 1) * 128]
            piece[half * 2 + c, PROMPT:, :] = square_rows
    all_group(lambda i, d: piece_copy(i, d).start())
    landed[seq, y_lo] = piece[y_lo * 2 + core]
    send_head_in(1)
    send_head_in(2)


    all_group(lambda i, d: piece_copy(i, d).wait_recv())
    for g in range(GROUP):
        rows = landed[0, g, PROMPT:, :].astype(F32)
        for s in range(1, SEQ):
            rows = rows + landed[s, g, PROMPT:, :].astype(F32)
        mean = jnp.sum(rows, axis=0, keepdims=True) * (1.0 / D_TEXT)
        inverse = lax.rsqrt(jnp.transpose(jnp.broadcast_to(mean, (128, 128))) + EPSILON)
        for s in range(SEQ):
            text[g * 128 : (g + 1) * 128, s * 128 : (s + 1) * 128] = (
                landed[s, g, :PROMPT, :].astype(F32) * inverse
            ).astype(BF)


    def project_kv(h):
        def arrived(i):
            for n in range(2):
                weight_copy(n, h, i).wait_recv()

        loop(1, ZS, arrived)
        for n in range(2):
            weight_own(n, h).wait()
        weights = wkv[h].reshape(ZS * 128, 256)
        kv_core[h] = nn(text[256:, :], weights).astype(BF)
        kv_core_copy(h).start()
        kv_own[h] = nn(text[:256, :], weights)

    def add_core(h):
        kv_core_copy(h).wait_recv()
        kv_own[h] += kv_core_in[h].astype(F32)
        kv_far[h] = kv_own[h, block128(1 - y_lo), :].astype(BF)
        kv_far_copy(h).start()

    loop(0, HEADS_HERE, project_kv)
    loop(0, HEADS_HERE, add_core)
    for g in range(GROUP):
        text_t[:, g * 128 : (g + 1) * 128] = jnp.transpose(text[g * 128 : (g + 1) * 128, :])


    length = length_ref[0]

    def attend(h, i):
        rows = pl.ds(pl.multiple_of(i * QUERY_BLOCK, QUERY_BLOCK), QUERY_BLOCK)
        queries, cotangent, keys, values = q[h, rows, :], do[h, rows, :], k[h], v[h]
        scores = nt(queries, keys)
        allowed = lax.broadcasted_iota(jnp.int32, (1, PROMPT), 1) < length
        scores = jnp.concatenate(
            [scores[:, :TOKENS], jnp.where(allowed, scores[:, TOKENS:], -jnp.inf)], axis=1
        )
        peak = jnp.max(scores, axis=1, keepdims=True)
        weights = jnp.exp2((scores - peak) * EXP2_SCALE)
        weights_low = weights.astype(BF)
        sums = nn(weights_low, jnp.concatenate([values, jnp.ones_like(values)], axis=1))
        inverse = 1.0 / sums[:, HEAD_DIM:]
        output = sums[:, :HEAD_DIM] * inverse
        out[h, rows, :] = output.astype(BF)
        cotangent_wide = cotangent.astype(F32)
        center = jnp.sum(cotangent_wide * output, axis=1, keepdims=True)
        score_grad = (weights * (nt(cotangent, values) - center)).astype(BF)
        scaled = inverse * SCALE
        dq[h, rows, :] = (nn(score_grad, keys) * scaled).astype(BF)
        dk_total[...] += tn(score_grad, (queries.astype(F32) * scaled).astype(BF))
        dv_total[...] += tn(weights_low, (cotangent_wide * inverse).astype(BF))

    def weight_grads(h):
        dkv_far(h).wait_recv()
        dkv_core(h, 1).start()
        dkv_core(h, 0).wait_recv()
        dkv_core(h, 1).wait_recv()
        products = nn(text_t[...], dkv_all[h].reshape(GROUP * 128, 256))
        grads[h] = products.astype(BF).reshape(ZS, 128, 256)
        loop(1, ZS, lambda i: grad_copy(h, i).start())

    def head(h):
        kv_far_copy(h).wait_recv()
        kv = kv_own[h, block128(y_lo), :] + kv_far_in[h].astype(F32)
        k[h, TOKENS:, :] = kv[:, :128].astype(BF)
        v[h, TOKENS:, :] = kv[:, 128:].astype(BF)
        for n in range(4):
            loop(1, SEQ, lambda d: in_copy(n, h, d).wait_recv())
            in_own(n, h).wait()
        dk_total[...] = jnp.zeros_like(dk_total)
        dv_total[...] = jnp.zeros_like(dv_total)
        loop(0, TOKENS // QUERY_BLOCK, lambda i: attend(h, i))
        dk[h] = dk_total[:TOKENS, :].astype(BF)
        dv[h] = dv_total[:TOKENS, :].astype(BF)
        dkv_all[h, y_lo] = jnp.concatenate(
            [dk_total[TOKENS:, :], dv_total[TOKENS:, :]], axis=1
        ).astype(BF)
        dkv_far(h).start()
        dkv_core(h, 0).start()
        for n in range(4):
            loop(1, SEQ, lambda d: out_copy(n, h, d).start())
            out_own(n, h).start()

        @pl.when(h > 0)
        def _():
            weight_grads(h - 1)

    loop(0, HEADS_HERE, head)
    weight_grads(HEADS_HERE - 1)
    for h in range(HEADS_HERE):
        total = grads[h, z].astype(F32)
        for i in range(1, ZS):
            grad_copy(h, i).wait_recv()
            total = total + grads_in[h, i].astype(F32)
        key_weight_grad[:, h * 128 : (h + 1) * 128] = total[:, :128]
        value_weight_grad[:, h * 128 : (h + 1) * 128] = total[:, 128:]


    def finish(h):
        for n in range(4):

            def each(d):
                out_copy(n, h, d).wait_recv()
                out_copy(n, h, d).wait_send()
                in_copy(n, h, d).wait_send()

            loop(1, SEQ, each)
            out_own(n, h).wait()
        kv_core_copy(h).wait_send()
        kv_far_copy(h).wait_send()
        dkv_far(h).wait_send()
        dkv_core(h, 0).wait_send()
        dkv_core(h, 1).wait_send()

        def finish_z(i):
            grad_copy(h, i).wait_send()
            for n in range(2):
                weight_copy(n, h, i).wait_send()

        loop(1, ZS, finish_z)

    loop(0, HEADS_HERE, finish)
    loop(1, SEQ, lambda d: part_copy(d).wait_send())
    all_group(lambda i, d: piece_copy(i, d).wait_send())


def hand_over(*refs):
    count = 6
    sources, targets, holds = refs[:count], refs[count : 2 * count], refs[2 * count : 3 * count]
    sem = refs[3 * count]
    parts = [(n, part) for part in range(2) for n in range(count)]

    def load(n, part):
        rows = pl.ds(part * 64, 64)
        return pltpu.make_async_copy(sources[n].at[rows], holds[n].at[rows], sem.at[0, n, part])

    def store(n, part):
        rows = pl.ds(part * 64, 64)
        return pltpu.make_async_copy(holds[n].at[rows], targets[n].at[rows], sem.at[1, n, part])

    for n, part in parts:
        load(n, part).start()
    for n, part in parts:
        load(n, part).wait()
        store(n, part).start()
    for n, part in parts:
        store(n, part).wait()


def body(
    text_context,
    text_residual,
    text_out_weight,
    text_gain,
    prompt_length,
    key_weight,
    value_weight,
    video_query,
    video_key,
    video_value,
    out_cotangent,
):
    vmem = pl.BlockSpec(memory_space=pltpu.VMEM)
    hbm = pl.BlockSpec(memory_space=pl.ANY)
    smem = pl.BlockSpec(memory_space=pltpu.SMEM)
    dma = pltpu.SemaphoreType.DMA
    tokens = jax.ShapeDtypeStruct((ROWS, SEQ * WIDTH), BF)
    weights = jax.ShapeDtypeStruct((128, WIDTH), F32)
    scratch = [
        pltpu.VMEM((HEADS_HERE, TOKENS, HEAD_DIM), BF),
        pltpu.VMEM((HEADS_HERE, ALL_ROWS, HEAD_DIM), BF),
        pltpu.VMEM((HEADS_HERE, ALL_ROWS, HEAD_DIM), BF),
        pltpu.VMEM((HEADS_HERE, TOKENS, HEAD_DIM), BF),
        pltpu.VMEM((HEADS_HERE, TOKENS, HEAD_DIM), BF),
        pltpu.VMEM((HEADS_HERE, TOKENS, HEAD_DIM), BF),
        pltpu.VMEM((HEADS_HERE, TOKENS, HEAD_DIM), BF),
        pltpu.VMEM((HEADS_HERE, TOKENS, HEAD_DIM), BF),
        pltpu.VMEM((ALL_ROWS, HEAD_DIM), F32),
        pltpu.VMEM((ALL_ROWS, HEAD_DIM), F32),
        pltpu.VMEM((SEQ, SHARE, SHARE), BF),
        pltpu.VMEM((PROMPT, SHARE), BF),
        pltpu.VMEM((PROMPT, SHARE), F32),
        pltpu.VMEM((SEQ, PROMPT, SHARE), BF),
        pltpu.VMEM((SEQ, PROMPT, SHARE), BF),
        pltpu.VMEM((GROUP, PROMPT + 16, 128), BF),
        pltpu.VMEM((SEQ, GROUP, PROMPT + 16, 128), BF),
        pltpu.VMEM((GROUP * PROMPT, SEQ * 128), BF),
        pltpu.VMEM((SEQ * 128, GROUP * PROMPT), BF),
        pltpu.VMEM((HEADS_HERE, ZS, 128, 256), BF),
        pltpu.VMEM((HEADS_HERE, 2 * PROMPT, 256), F32),
        pltpu.VMEM((HEADS_HERE, 2 * PROMPT, 256), BF),
        pltpu.VMEM((HEADS_HERE, 2 * PROMPT, 256), BF),
        pltpu.VMEM((HEADS_HERE, PROMPT, 256), BF),
        pltpu.VMEM((HEADS_HERE, PROMPT, 256), BF),
        pltpu.VMEM((HEADS_HERE, GROUP, PROMPT, 256), BF),
        pltpu.VMEM((HEADS_HERE, ZS, 128, 256), BF),
        pltpu.VMEM((HEADS_HERE, ZS, 128, 256), BF),
        dma((4, HEADS_HERE, SEQ)),
        dma((4, HEADS_HERE, SEQ)),
        dma((4, HEADS_HERE, SEQ)),
        dma((4, HEADS_HERE, SEQ)),
        dma((2, HEADS_HERE, ZS)),
        dma((2, HEADS_HERE, ZS)),
        dma((SEQ,)),
        dma((SEQ,)),
        dma((SEQ, 2)),
        dma((2,)),
        dma((GROUP, SEQ)),
        dma((GROUP, SEQ)),
        dma((HEADS_HERE,)),
        dma((HEADS_HERE,)),
        dma((HEADS_HERE,)),
        dma((HEADS_HERE,)),
        dma((HEADS_HERE, 3)),
        dma((HEADS_HERE, 3)),
        dma((HEADS_HERE, ZS)),
        dma((HEADS_HERE, ZS)),
    ]
    shapes = [tokens] * 4 + [weights] * 2
    made = pl.pallas_call(
        kernel,
        out_shape=shapes,
        in_specs=[smem, vmem, vmem] + [hbm] * 8,
        out_specs=[hbm] * 4 + [vmem] * 2,
        scratch_shapes=scratch,
        name="joint_attention",
        compiler_params=pltpu.CompilerParams(
            collective_id=0, has_side_effects=True, vmem_limit_bytes=56 * 1024 * 1024
        ),
    )(
        prompt_length,
        text_context[0],
        text_gain.reshape(1, D_TEXT),
        text_residual[0],
        text_out_weight,
        key_weight,
        value_weight,
        video_query[0],
        video_key[0],
        video_value[0],
        out_cotangent[0],
    )
    attended, query_grad, key_grad, value_grad, key_weight_grad, value_weight_grad = pl.pallas_call(
        hand_over,
        out_shape=shapes,
        in_specs=[hbm] * 6,
        out_specs=[hbm] * 6,
        scratch_shapes=[pltpu.VMEM(x.shape, x.dtype) for x in shapes] + [dma((2, 6, 2))],
        name="hand_over",
    )(*made)
    return (
        attended[None],
        query_grad[None],
        key_grad[None],
        value_grad[None],
        key_weight_grad,
        value_weight_grad,
    )


def solution(mesh):
    in_specs = (
        P("dp", None, "seq"),
        P("dp", None, None),
        P("seq", None),
        P(),
        P("dp"),
        P("dp", "seq"),
        P("dp", "seq"),
        P("dp", "seq", None),
        P("dp", "seq", None),
        P("dp", "seq", None),
        P("dp", "seq", None),
    )
    out_specs = (
        P("dp", "seq", None),
        P("dp", "seq", None),
        P("dp", "seq", None),
        P("dp", "seq", None),
        P("dp", "seq"),
        P("dp", "seq"),
    )
    return jax.shard_map(body, mesh=mesh, in_specs=in_specs, out_specs=out_specs, check_vma=False)
```

profile of v0, /device:TPU:1, one launch (start us, length us, event | category | flops | bytes accessed | tf_op | source)
XLA Modules:
  0.0 144.5 jit_solution(11765782166393223053)
XLA Ops:
  1.3 140.3 %joint_attention.1 = (bf16[128,3072]{1,0:T(8,128)(2,1)}, bf16[128,3072]{1,0:T(8,128)(2,1)}, bf16[128,3072]{1,0:T(8,128)(2,1)}, bf16[128,3072]{1,0:T(8,128)(2,1)}...) custom-call(s32[1]{0:T(128)S(6)} %copy.17.length_ref, bf16[128,512]{1,0:T(8,128)(2,1)} %bitcast.16, f32[1,4096]{1,0:T(1,128)} %bitcast.17, ...), custom_call_target="tpu_custom_call" | custom-call | tf_op jit(solution)/shard_map/joint_attention/pallas_call | solution.py:571
  141.6 3.0 %hand_over.1 = (bf16[128,3072]{1,0:T(8,128)(2,1)}, bf16[128,3072]{1,0:T(8,128)(2,1)}, bf16[128,3072]{1,0:T(8,128)(2,1)}, bf16[128,3072]{1,0:T(8,128)(2,1)}, f32[128,384]{1,0:T(8,128)}, /*index=5*/f32[128,384]{1,0:T(8,128)}) custom-call(bf16[128,3072]{1,0:T(8,128)(2,1)} %get-tuple-element.18.refs_0_, bf16[128,3072]{1,0:T(8,128)(2,1)} %get-tuple-element.19.refs_1_, ...), custom_call_target="tpu_custom_call" | custom-call | tf_op jit(solution)/shard_map/hand_over/pallas_call | solution.py:594
where the time goes:
time: 145 us
  Pallas kernels  143 us (99%)
    pallas_call x1, Pallas kernels, body(): pl.pallas_call(kernel, out_shape=shapes, in_specs=[smem, vmem, vmem] + [h...  140 us
    pallas_call x1, Pallas kernels, body(): pl.pallas_call(hand_over, out_shape=shapes, in_specs=[hbm] * 6, out_specs...  2.98 us

commit v1 on v0

--- a/solution.py
+++ b/solution.py
@@ -47,8 +47,8 @@
 
 def kernel(
     length_ref,
-    context,
-    gain,
+    context_hbm,
+    gain_hbm,
     residual,
     out_weight,
     key_weight,
@@ -91,6 +91,11 @@
     dkv_all,
     grads,
     grads_in,
+    grads_passed,
+    grads_sum,
+    total_grads,
+    context,
+    gain,
     in_s,
     in_r,
     out_s,
@@ -111,6 +116,8 @@
     dk_r,
     wg_s,
     wg_r,
+    grad_sem,
+    small_sem,
 ):
     dp = lax.axis_index("dp")
     seq = lax.axis_index("seq")
@@ -147,6 +154,10 @@
             return carry
 
         lax.fori_loop(low, high, run, 0)
+
+    def each(low, high, step):
+        for i in range(low, high):
+            step(i)
 
 
     def w_load(d, half):
@@ -187,8 +198,8 @@
         return remote(
             sources[n].at[:, block128(peer[1] * HEADS_HERE + h)],
             landings[n].at[h, block128(seq)],
-            in_s.at[n, h, d],
-            in_r.at[n, h, d],
+            in_s.at[n, h],
+            in_r.at[n, h],
             peer,
         )
 
@@ -196,7 +207,7 @@
         return pltpu.make_async_copy(
             sources[n].at[:, block128(seq * HEADS_HERE + h)],
             landings[n].at[h, block128(seq)],
-            in_r.at[n, h, 0],
+            in_r.at[n, h],
         )
 
     def out_copy(n, h, d):
@@ -204,8 +215,8 @@
         return remote(
             results[n].at[h, block128(peer[1])],
             targets[n].at[:, block128(seq * HEADS_HERE + h)],
-            out_s.at[n, h, d],
-            out_r.at[n, h, d],
+            out_s.at[n, h],
+            out_r.at[n, h],
             peer,
         )
 
@@ -213,8 +224,25 @@
         return pltpu.make_async_copy(
             results[n].at[h, block128(seq)],
             targets[n].at[:, block128(seq * HEADS_HERE + h)],
-            out_r.at[n, h, 0],
-        )
+            out_r.at[n, h],
+        )
+
+
+    def all_in(n, h):
+        rows = landings[n].at[h, pl.ds(0, TOKENS)]
+        return pltpu.make_async_copy(rows, rows, in_r.at[n, h])
+
+    def all_in_sent(n, h):
+        rows = landings[n].at[h, pl.ds(0, TOKENS - ROWS)]
+        return pltpu.make_async_copy(rows, rows, in_s.at[n, h])
+
+    def all_out(n, h):
+        rows = results[n].at[h]
+        return pltpu.make_async_copy(rows, rows, out_r.at[n, h])
+
+    def all_out_sent(n, h):
+        rows = results[n].at[h, pl.ds(0, TOKENS - ROWS)]
+        return pltpu.make_async_copy(rows, rows, out_s.at[n, h])
 
     def part_copy(d):
         return remote(part.at[d], part_in.at[d], rs_s.at[d], rs_r.at[d], seq_peer(d))
@@ -249,16 +277,35 @@
             core_peer(),
         )
 
-    def grad_copy(h, i):
-        return remote(grads.at[h, (z + i) % 8], grads_in.at[h, i], wg_s.at[h, i], wg_r.at[h, i], z_peer(i))
+    def grad_near(h, n):
+        step = (1, ZS - 1)[n]
+        return remote(
+            grads.at[h, (z + step) % 8], grads_in.at[h, n], wg_s.at[h, n], wg_r.at[h, n], z_peer(step)
+        )
+
+    def grad_passed(h, n):
+        block, step = ((3, 1), (ZS - 3, ZS - 1), (4, 2))[n]
+        return remote(
+            grads.at[h, (z + block) % 8],
+            grads_passed.at[h, n],
+            wg_s.at[h, 2 + n],
+            wg_r.at[h, 2 + n],
+            z_peer(step),
+        )
+
+    def grad_far(h, n):
+        step = (2, ZS - 2)[n]
+        return remote(
+            grads_sum.at[h, n], grads_in.at[h, 2 + n], wg_s.at[h, 5 + n], wg_r.at[h, 5 + n], z_peer(step)
+        )
 
     def send_head_in(h):
         for n in range(4):
-            loop(1, SEQ, lambda d: in_copy(n, h, d).start())
+            each(1, SEQ, lambda d: in_copy(n, h, d).start())
 
     def all_group(step):
-        loop(1, SEQ, lambda d: step(0, d))
-        loop(1, GROUP, lambda i: loop(0, SEQ, lambda d: step(i, d)))
+        each(1, SEQ, lambda d: step(0, d))
+        each(1, GROUP, lambda i: each(0, SEQ, lambda d: step(i, d)))
 
 
     barrier = pltpu.get_barrier_semaphore()
@@ -267,15 +314,20 @@
         pl.semaphore_signal(barrier, inc=1, device_id=peer, device_id_type=MESH)
 
     all_group(lambda i, d: greet(group_peer(i, d)))
-    loop(1, ZS, lambda i: greet(z_peer(i)))
+    each(1, ZS, lambda i: greet(z_peer(i)))
+
+    context_load = pltpu.make_async_copy(context_hbm, context, small_sem.at[0])
+    gain_load = pltpu.make_async_copy(gain_hbm, gain, small_sem.at[1])
+    context_load.start()
 
     def start_loads(d):
         for half in range(2):
             w_load(d, half).start()
 
-    loop(0, SEQ, start_loads)
+    each(0, SEQ, start_loads)
     for half in range(2):
         res_load(half).start()
+    gain_load.start()
     for h in range(HEADS_HERE):
         for n in range(2):
             weight_own(n, h).start()
@@ -288,6 +340,8 @@
             w_load(d, half).wait()
         return nn(context[...], w_out[d])
 
+    context_load.wait()
+    gain_load.wait()
     for half in range(2):
         res_load(half).wait()
     summed[...] = project(0) + res[...].astype(F32)
@@ -295,13 +349,13 @@
     def project_step(d):
         part[d] = project(d).astype(BF)
 
-    loop(1, SEQ, project_step)
+    each(1, SEQ, project_step)
     pl.semaphore_wait(barrier, GROUP * SEQ - 1 + ZS - 1)
-    loop(1, SEQ, lambda d: part_copy(d).start())
+    each(1, SEQ, lambda d: part_copy(d).start())
 
     def send_weights(h):
         for n in range(2):
-            loop(1, ZS, lambda i: weight_copy(n, h, i).start())
+            each(1, ZS, lambda i: weight_copy(n, h, i).start())
 
     send_weights(0)
     send_head_in(0)
@@ -335,7 +389,6 @@
     all_group(lambda i, d: piece_copy(i, d).start())
     landed[seq, y_lo] = piece[y_lo * 2 + core]
     send_head_in(1)
-    send_head_in(2)
 
 
     all_group(lambda i, d: piece_copy(i, d).wait_recv())
@@ -356,7 +409,7 @@
             for n in range(2):
                 weight_copy(n, h, i).wait_recv()
 
-        loop(1, ZS, arrived)
+        each(1, ZS, arrived)
         for n in range(2):
             weight_own(n, h).wait()
         weights = wkv[h].reshape(ZS * 128, 256)
@@ -372,6 +425,7 @@
 
     loop(0, HEADS_HERE, project_kv)
     loop(0, HEADS_HERE, add_core)
+    send_head_in(2)
     for g in range(GROUP):
         text_t[:, g * 128 : (g + 1) * 128] = jnp.transpose(text[g * 128 : (g + 1) * 128, :])
 
@@ -401,14 +455,30 @@
         dk_total[...] += tn(score_grad, (queries.astype(F32) * scaled).astype(BF))
         dv_total[...] += tn(weights_low, (cotangent_wide * inverse).astype(BF))
 
-    def weight_grads(h):
+    def dkv_forward(h):
         dkv_far(h).wait_recv()
         dkv_core(h, 1).start()
+
+    def weight_grads(h):
         dkv_core(h, 0).wait_recv()
         dkv_core(h, 1).wait_recv()
         products = nn(text_t[...], dkv_all[h].reshape(GROUP * 128, 256))
         grads[h] = products.astype(BF).reshape(ZS, 128, 256)
-        loop(1, ZS, lambda i: grad_copy(h, i).start())
+        for n in range(3):
+            grad_passed(h, n).start()
+        for n in range(2):
+            grad_near(h, n).start()
+
+
+    def pass_grads(h):
+        for n in range(3):
+            grad_passed(h, n).wait_recv()
+        up = grads[h, (z + 2) % 8].astype(F32) + grads_passed[h, 0].astype(F32)
+        grads_sum[h, 0] = (up + grads_passed[h, 2].astype(F32)).astype(BF)
+        down = grads[h, (z + ZS - 2) % 8].astype(F32) + grads_passed[h, 1].astype(F32)
+        grads_sum[h, 1] = down.astype(BF)
+        for n in range(2):
+            grad_far(h, n).start()
 
     def head(h):
         kv_far_copy(h).wait_recv()
@@ -416,11 +486,16 @@
         k[h, TOKENS:, :] = kv[:, :128].astype(BF)
         v[h, TOKENS:, :] = kv[:, 128:].astype(BF)
         for n in range(4):
-            loop(1, SEQ, lambda d: in_copy(n, h, d).wait_recv())
-            in_own(n, h).wait()
+            all_in(n, h).wait()
         dk_total[...] = jnp.zeros_like(dk_total)
         dv_total[...] = jnp.zeros_like(dv_total)
-        loop(0, TOKENS // QUERY_BLOCK, lambda i: attend(h, i))
+        attend(h, 0)
+
+        @pl.when(h > 0)
+        def _():
+            dkv_forward(h - 1)
+
+        attend(h, 1)
         dk[h] = dk_total[:TOKENS, :].astype(BF)
         dv[h] = dv_total[:TOKENS, :].astype(BF)
         dkv_all[h, y_lo] = jnp.concatenate(
@@ -429,50 +504,68 @@
         dkv_far(h).start()
         dkv_core(h, 0).start()
         for n in range(4):
-            loop(1, SEQ, lambda d: out_copy(n, h, d).start())
+            each(1, SEQ, lambda d: out_copy(n, h, d).start())
             out_own(n, h).start()
 
         @pl.when(h > 0)
         def _():
             weight_grads(h - 1)
 
+        @pl.when(h > 1)
+        def _():
+            pass_grads(h - 2)
+
     loop(0, HEADS_HERE, head)
+    dkv_forward(HEADS_HERE - 1)
+    pass_grads(HEADS_HERE - 2)
     weight_grads(HEADS_HERE - 1)
+    pass_grads(HEADS_HERE - 1)
+
+    def grads_out(n):
+        return pltpu.make_async_copy(
+            total_grads.at[n], (key_weight_grad, value_weight_grad)[n], grad_sem.at[n]
+        )
+
     for h in range(HEADS_HERE):
         total = grads[h, z].astype(F32)
-        for i in range(1, ZS):
-            grad_copy(h, i).wait_recv()
-            total = total + grads_in[h, i].astype(F32)
-        key_weight_grad[:, h * 128 : (h + 1) * 128] = total[:, :128]
-        value_weight_grad[:, h * 128 : (h + 1) * 128] = total[:, 128:]
+        for n in range(2):
+            grad_near(h, n).wait_recv()
+            grad_far(h, n).wait_recv()
+            total = total + grads_in[h, n].astype(F32) + grads_in[h, 2 + n].astype(F32)
+        for n in range(2):
+            total_grads[n, :, h * 128 : (h + 1) * 128] = total[:, n * 128 : (n + 1) * 128]
+    for n in range(2):
+        grads_out(n).start()
 
 
     def finish(h):
         for n in range(4):
-
-            def each(d):
-                out_copy(n, h, d).wait_recv()
-                out_copy(n, h, d).wait_send()
-                in_copy(n, h, d).wait_send()
-
-            loop(1, SEQ, each)
-            out_own(n, h).wait()
+            all_out(n, h).wait()
+            all_out_sent(n, h).wait()
+            all_in_sent(n, h).wait()
         kv_core_copy(h).wait_send()
         kv_far_copy(h).wait_send()
         dkv_far(h).wait_send()
         dkv_core(h, 0).wait_send()
         dkv_core(h, 1).wait_send()
 
+        for n in range(3):
+            grad_passed(h, n).wait_send()
+        for n in range(2):
+            grad_near(h, n).wait_send()
+            grad_far(h, n).wait_send()
+
         def finish_z(i):
-            grad_copy(h, i).wait_send()
             for n in range(2):
                 weight_copy(n, h, i).wait_send()
 
-        loop(1, ZS, finish_z)
+        each(1, ZS, finish_z)
 
     loop(0, HEADS_HERE, finish)
-    loop(1, SEQ, lambda d: part_copy(d).wait_send())
+    each(1, SEQ, lambda d: part_copy(d).wait_send())
     all_group(lambda i, d: piece_copy(i, d).wait_send())
+    for n in range(2):
+        grads_out(n).wait()
 
 
 def hand_over(*refs):
@@ -511,7 +604,6 @@
     video_value,
     out_cotangent,
 ):
-    vmem = pl.BlockSpec(memory_space=pltpu.VMEM)
     hbm = pl.BlockSpec(memory_space=pl.ANY)
     smem = pl.BlockSpec(memory_space=pltpu.SMEM)
     dma = pltpu.SemaphoreType.DMA
@@ -545,11 +637,16 @@
         pltpu.VMEM((HEADS_HERE, PROMPT, 256), BF),
         pltpu.VMEM((HEADS_HERE, GROUP, PROMPT, 256), BF),
         pltpu.VMEM((HEADS_HERE, ZS, 128, 256), BF),
-        pltpu.VMEM((HEADS_HERE, ZS, 128, 256), BF),
-        dma((4, HEADS_HERE, SEQ)),
-        dma((4, HEADS_HERE, SEQ)),
-        dma((4, HEADS_HERE, SEQ)),
-        dma((4, HEADS_HERE, SEQ)),
+        pltpu.VMEM((HEADS_HERE, 4, 128, 256), BF),
+        pltpu.VMEM((HEADS_HERE, 3, 128, 256), BF),
+        pltpu.VMEM((HEADS_HERE, 2, 128, 256), BF),
+        pltpu.VMEM((2, 128, WIDTH), F32),
+        pltpu.VMEM((PROMPT, SHARE), BF),
+        pltpu.VMEM((1, D_TEXT), F32),
+        dma((4, HEADS_HERE)),
+        dma((4, HEADS_HERE)),
+        dma((4, HEADS_HERE)),
+        dma((4, HEADS_HERE)),
         dma((2, HEADS_HERE, ZS)),
         dma((2, HEADS_HERE, ZS)),
         dma((SEQ,)),
@@ -564,15 +661,17 @@
         dma((HEADS_HERE,)),
         dma((HEADS_HERE, 3)),
         dma((HEADS_HERE, 3)),
-        dma((HEADS_HERE, ZS)),
-        dma((HEADS_HERE, ZS)),
+        dma((HEADS_HERE, 7)),
+        dma((HEADS_HERE, 7)),
+        dma((2,)),
+        dma((2,)),
     ]
     shapes = [tokens] * 4 + [weights] * 2
     made = pl.pallas_call(
         kernel,
         out_shape=shapes,
-        in_specs=[smem, vmem, vmem] + [hbm] * 8,
-        out_specs=[hbm] * 4 + [vmem] * 2,
+        in_specs=[smem] + [hbm] * 10,
+        out_specs=[hbm] * 6,
         scratch_shapes=scratch,
         name="joint_attention",
         compiler_params=pltpu.CompilerParams(

time: 145 us -> 133 us (0.917)
  Pallas kernels: 143 us -> 132 us
    pallas_call x1, Pallas kernels: 140 us -> 129 us  [body(): pl.pallas_call(kernel, out_shape=shapes, in_specs=[smem] + [hbm] * 10, ou...]
where the time goes in v1:
time: 133 us
  Pallas kernels  132 us (99%)
    pallas_call x1, Pallas kernels, body(): pl.pallas_call(kernel, out_shape=shapes, in_specs=[smem] + [hbm] * 10, ou...  129 us
    pallas_call x1, Pallas kernels, body(): pl.pallas_call(hand_over, out_shape=shapes, in_specs=[hbm] * 6, out_specs...  2.98 us

profile of v1, /device:TPU:1, one launch (start us, length us, event | category | flops | bytes accessed | tf_op | source)
XLA Modules:
  0.0 132.9 jit_solution(14023838898520940741)
XLA Ops:
  1.3 128.6 %joint_attention.1 = (bf16[128,3072]{1,0:T(8,128)(2,1)}, bf16[128,3072]{1,0:T(8,128)(2,1)}, bf16[128,3072]{1,0:T(8,128)(2,1)}, bf16[128,3072]{1,0:T(8,128)(2,1)}...) custom-call(s32[1]{0:T(128)S(6)} %copy.17.length_ref, bf16[128,512]{1,0:T(8,128)(2,1)} %bitcast.16, f32[1,4096]{1,0:T(1,128)} %bitcast.17, ...), custom_call_target="tpu_custom_call" | custom-call | tf_op jit(solution)/shard_map/joint_attention/pallas_call | solution.py:670
  129.9 3.0 %hand_over.1 = (bf16[128,3072]{1,0:T(8,128)(2,1)}, bf16[128,3072]{1,0:T(8,128)(2,1)}, bf16[128,3072]{1,0:T(8,128)(2,1)}, bf16[128,3072]{1,0:T(8,128)(2,1)}, f32[128,384]{1,0:T(8,128)}, /*index=5*/f32[128,384]{1,0:T(8,128)}) custom-call(bf16[128,3072]{1,0:T(8,128)(2,1)} %get-tuple-element.18.refs_0_, bf16[128,3072]{1,0:T(8,128)(2,1)} %get-tuple-element.19.refs_1_, ...), custom_call_target="tpu_custom_call" | custom-call | tf_op jit(solution)/shard_map/hand_over/pallas_call | solution.py:693

commit v2 on v1

--- a/solution.py
+++ b/solution.py
@@ -284,10 +284,16 @@
         )
 
     def grad_passed(h, n):
-        block, step = ((3, 1), (ZS - 3, ZS - 1), (4, 2))[n]
+        block, step, low, high = (
+            (3, 1, 0, 128),
+            (ZS - 3, ZS - 1, 0, 128),
+            (4, 2, 0, 64),
+            (4, ZS - 2, 64, 128),
+        )[n]
+        rows = pl.ds(low, high - low)
         return remote(
-            grads.at[h, (z + block) % 8],
-            grads_passed.at[h, n],
+            grads.at[h, (z + block) % 8, rows],
+            grads_passed.at[h, n, rows],
             wg_s.at[h, 2 + n],
             wg_r.at[h, 2 + n],
             z_peer(step),
@@ -296,7 +302,7 @@
     def grad_far(h, n):
         step = (2, ZS - 2)[n]
         return remote(
-            grads_sum.at[h, n], grads_in.at[h, 2 + n], wg_s.at[h, 5 + n], wg_r.at[h, 5 + n], z_peer(step)
+            grads_sum.at[h, n], grads_in.at[h, 2 + n], wg_s.at[h, 6 + n], wg_r.at[h, 6 + n], z_peer(step)
         )
 
     def send_head_in(h):
@@ -464,21 +470,28 @@
         dkv_core(h, 1).wait_recv()
         products = nn(text_t[...], dkv_all[h].reshape(GROUP * 128, 256))
         grads[h] = products.astype(BF).reshape(ZS, 128, 256)
-        for n in range(3):
+        for n in range(4):
             grad_passed(h, n).start()
         for n in range(2):
             grad_near(h, n).start()
 
 
     def pass_grads(h):
-        for n in range(3):
+        for n in range(4):
             grad_passed(h, n).wait_recv()
         up = grads[h, (z + 2) % 8].astype(F32) + grads_passed[h, 0].astype(F32)
-        grads_sum[h, 0] = (up + grads_passed[h, 2].astype(F32)).astype(BF)
+        grads_sum[h, 0, :64] = (up[:64] + grads_passed[h, 2, :64].astype(F32)).astype(BF)
+        grads_sum[h, 0, 64:] = up[64:].astype(BF)
         down = grads[h, (z + ZS - 2) % 8].astype(F32) + grads_passed[h, 1].astype(F32)
-        grads_sum[h, 1] = down.astype(BF)
+        grads_sum[h, 1, :64] = down[:64].astype(BF)
+        grads_sum[h, 1, 64:] = (down[64:] + grads_passed[h, 3, 64:].astype(F32)).astype(BF)
         for n in range(2):
             grad_far(h, n).start()
+
+    def send_head_out(h, arrays):
+        for n in arrays:
+            each(1, SEQ, lambda d: out_copy(n, h, d).start())
+            out_own(n, h).start()
 
     def head(h):
         kv_far_copy(h).wait_recv()
@@ -503,9 +516,14 @@
         ).astype(BF)
         dkv_far(h).start()
         dkv_core(h, 0).start()
-        for n in range(4):
-            each(1, SEQ, lambda d: out_copy(n, h, d).start())
-            out_own(n, h).start()
+
+        @pl.when(h < HEADS_HERE - 1)
+        def _():
+            send_head_out(h, range(4))
+
+        @pl.when(h < HEADS_HERE - 2)
+        def _():
+            send_head_out(h, range(4, 4))
 
         @pl.when(h > 0)
         def _():
@@ -517,8 +535,9 @@
 
     loop(0, HEADS_HERE, head)
     dkv_forward(HEADS_HERE - 1)
+    send_head_out(HEADS_HERE - 1, range(4))
+    weight_grads(HEADS_HERE - 1)
     pass_grads(HEADS_HERE - 2)
-    weight_grads(HEADS_HERE - 1)
     pass_grads(HEADS_HERE - 1)
 
     def grads_out(n):
@@ -549,7 +568,7 @@
         dkv_core(h, 0).wait_send()
         dkv_core(h, 1).wait_send()
 
-        for n in range(3):
+        for n in range(4):
             grad_passed(h, n).wait_send()
         for n in range(2):
             grad_near(h, n).wait_send()
@@ -638,7 +657,7 @@
         pltpu.VMEM((HEADS_HERE, GROUP, PROMPT, 256), BF),
         pltpu.VMEM((HEADS_HERE, ZS, 128, 256), BF),
         pltpu.VMEM((HEADS_HERE, 4, 128, 256), BF),
-        pltpu.VMEM((HEADS_HERE, 3, 128, 256), BF),
+        pltpu.VMEM((HEADS_HERE, 4, 128, 256), BF),
         pltpu.VMEM((HEADS_HERE, 2, 128, 256), BF),
         pltpu.VMEM((2, 128, WIDTH), F32),
         pltpu.VMEM((PROMPT, SHARE), BF),
@@ -661,8 +680,8 @@
         dma((HEADS_HERE,)),
         dma((HEADS_HERE, 3)),
         dma((HEADS_HERE, 3)),
-        dma((HEADS_HERE, 7)),
-        dma((HEADS_HERE, 7)),
+        dma((HEADS_HERE, 8)),
+        dma((HEADS_HERE, 8)),
         dma((2,)),
         dma((2,)),
     ]

time: 133 us -> 126 us (0.947)
  Pallas kernels: 132 us -> 125 us
    pallas_call x1, Pallas kernels: 129 us -> 122 us  [body(): pl.pallas_call(kernel, out_shape=shapes, in_specs=[smem] + [hbm] * 10, ou...]
where the time goes in v2:
time: 126 us
  Pallas kernels  125 us (99%)
  between operations  1.29 us (1%)
    pallas_call x1, Pallas kernels, body(): pl.pallas_call(kernel, out_shape=shapes, in_specs=[smem] + [hbm] * 10, ou...  122 us
    pallas_call x1, Pallas kernels, body(): pl.pallas_call(hand_over, out_shape=shapes, in_specs=[hbm] * 6, out_specs...  2.98 us

profile of v2, /device:TPU:1, one launch (start us, length us, event | category | flops | bytes accessed | tf_op | source)
XLA Modules:
  0.0 126.1 jit_solution(1470793521285850281)
XLA Ops:
  1.3 121.8 %joint_attention.1 = (bf16[128,3072]{1,0:T(8,128)(2,1)}, bf16[128,3072]{1,0:T(8,128)(2,1)}, bf16[128,3072]{1,0:T(8,128)(2,1)}, bf16[128,3072]{1,0:T(8,128)(2,1)}...) custom-call(s32[1]{0:T(128)S(6)} %copy.17.length_ref, bf16[128,512]{1,0:T(8,128)(2,1)} %bitcast.16, f32[1,4096]{1,0:T(1,128)} %bitcast.17, ...), custom_call_target="tpu_custom_call" | custom-call | tf_op jit(solution)/shard_map/joint_attention/pallas_call | solution.py:689
  123.1 3.0 %hand_over.1 = (bf16[128,3072]{1,0:T(8,128)(2,1)}, bf16[128,3072]{1,0:T(8,128)(2,1)}, bf16[128,3072]{1,0:T(8,128)(2,1)}, bf16[128,3072]{1,0:T(8,128)(2,1)}, f32[128,384]{1,0:T(8,128)}, /*index=5*/f32[128,384]{1,0:T(8,128)}) custom-call(bf16[128,3072]{1,0:T(8,128)(2,1)} %get-tuple-element.18.refs_0_, bf16[128,3072]{1,0:T(8,128)(2,1)} %get-tuple-element.19.refs_1_, ...), custom_call_target="tpu_custom_call" | custom-call | tf_op jit(solution)/shard_map/hand_over/pallas_call | solution.py:712

commit v3 on v2

--- a/solution.py
+++ b/solution.py
@@ -247,6 +247,10 @@
     def part_copy(d):
         return remote(part.at[d], part_in.at[d], rs_s.at[d], rs_r.at[d], seq_peer(d))
 
+    def part_piece(d, c):
+        rows = pl.ds(c * 32, 32)
+        return remote(part.at[d, rows], part_in.at[d, rows], rs_s.at[d], rs_r.at[d], seq_peer(d))
+
     def piece_copy(i, d):
         target = ((y_lo + i // 2) % 2) * 2 + (core + i % 2) % 2
         return remote(
@@ -357,14 +361,15 @@
 
     each(1, SEQ, project_step)
     pl.semaphore_wait(barrier, GROUP * SEQ - 1 + ZS - 1)
-    each(1, SEQ, lambda d: part_copy(d).start())
+    for c in range(4):
+        each(1, SEQ, lambda d: part_piece(d, c).start())
 
     def send_weights(h):
         for n in range(2):
             each(1, ZS, lambda i: weight_copy(n, h, i).start())
 
+    send_head_in(0)
     send_weights(0)
-    send_head_in(0)
     send_weights(1)
     send_weights(2)
 

time: 126 us -> 125 us (level)
  no operation moved by 1% of the time
where the time goes in v3:
time: 125 us
  Pallas kernels  124 us (99%)
  between operations  1.29 us (1%)
    pallas_call x1, Pallas kernels, body(): pl.pallas_call(kernel, out_shape=shapes, in_specs=[smem] + [hbm] * 10, ou...  121 us
    pallas_call x1, Pallas kernels, body(): pl.pallas_call(hand_over, out_shape=shapes, in_specs=[hbm] * 6, out_specs...  2.98 us

profile of v3, /device:TPU:1, one launch (start us, length us, event | category | flops | bytes accessed | tf_op | source)
XLA Modules:
  0.0 125.1 jit_solution(15535153490612646690)
XLA Ops:
  1.3 120.8 %joint_attention.1 = (bf16[128,3072]{1,0:T(8,128)(2,1)}, bf16[128,3072]{1,0:T(8,128)(2,1)}, bf16[128,3072]{1,0:T(8,128)(2,1)}, bf16[128,3072]{1,0:T(8,128)(2,1)}...) custom-call(s32[1]{0:T(128)S(6)} %copy.17.length_ref, bf16[128,512]{1,0:T(8,128)(2,1)} %bitcast.16, f32[1,4096]{1,0:T(1,128)} %bitcast.17, ...), custom_call_target="tpu_custom_call" | custom-call | tf_op jit(solution)/shard_map/joint_attention/pallas_call | solution.py:694
  122.1 3.0 %hand_over.1 = (bf16[128,3072]{1,0:T(8,128)(2,1)}, bf16[128,3072]{1,0:T(8,128)(2,1)}, bf16[128,3072]{1,0:T(8,128)(2,1)}, bf16[128,3072]{1,0:T(8,128)(2,1)}, f32[128,384]{1,0:T(8,128)}, /*index=5*/f32[128,384]{1,0:T(8,128)}) custom-call(bf16[128,3072]{1,0:T(8,128)(2,1)} %get-tuple-element.18.refs_0_, bf16[128,3072]{1,0:T(8,128)(2,1)} %get-tuple-element.19.refs_1_, ...), custom_call_target="tpu_custom_call" | custom-call | tf_op jit(solution)/shard_map/hand_over/pallas_call | solution.py:717

commit v4 on v3

--- a/solution.py
+++ b/solution.py
@@ -434,8 +434,14 @@
         kv_far[h] = kv_own[h, block128(1 - y_lo), :].astype(BF)
         kv_far_copy(h).start()
 
-    loop(0, HEADS_HERE, project_kv)
-    loop(0, HEADS_HERE, add_core)
+    project_kv(0)
+
+    def next_kv(h):
+        project_kv(h)
+        add_core(h - 1)
+
+    loop(1, HEADS_HERE, next_kv)
+    add_core(HEADS_HERE - 1)
     send_head_in(2)
     for g in range(GROUP):
         text_t[:, g * 128 : (g + 1) * 128] = jnp.transpose(text[g * 128 : (g + 1) * 128, :])
@@ -596,14 +602,14 @@
     count = 6
     sources, targets, holds = refs[:count], refs[count : 2 * count], refs[2 * count : 3 * count]
     sem = refs[3 * count]
-    parts = [(n, part) for part in range(2) for n in range(count)]
+    parts = [(n, part) for part in range(4) for n in range(count)]
 
     def load(n, part):
-        rows = pl.ds(part * 64, 64)
+        rows = pl.ds(part * 32, 32)
         return pltpu.make_async_copy(sources[n].at[rows], holds[n].at[rows], sem.at[0, n, part])
 
     def store(n, part):
-        rows = pl.ds(part * 64, 64)
+        rows = pl.ds(part * 32, 32)
         return pltpu.make_async_copy(holds[n].at[rows], targets[n].at[rows], sem.at[1, n, part])
 
     for n, part in parts:
@@ -719,7 +725,7 @@
         out_shape=shapes,
         in_specs=[hbm] * 6,
         out_specs=[hbm] * 6,
-        scratch_shapes=[pltpu.VMEM(x.shape, x.dtype) for x in shapes] + [dma((2, 6, 2))],
+        scratch_shapes=[pltpu.VMEM(x.shape, x.dtype) for x in shapes] + [dma((2, 6, 4))],
         name="hand_over",
     )(*made)
     return (

time: 125 us -> 127 us (1.016)
  no operation moved by 1% of the time
where the time goes in v4:
time: 127 us
  Pallas kernels  125 us (98%)
  between operations  1.45 us (1%)
    pallas_call x1, Pallas kernels, body(): pl.pallas_call(kernel, out_shape=shapes, in_specs=[smem] + [hbm] * 10, ou...  122 us
    pallas_call x1, Pallas kernels, body(): pl.pallas_call(hand_over, out_shape=shapes, in_specs=[hbm] * 6, out_specs...  3.65 us

profile of v4, /device:TPU:1, one launch (start us, length us, event | category | flops | bytes accessed | tf_op | source)
XLA Modules:
  0.0 126.8 jit_solution(18237527269056474831)
XLA Ops:
  1.3 121.7 %joint_attention.1 = (bf16[128,3072]{1,0:T(8,128)(2,1)}, bf16[128,3072]{1,0:T(8,128)(2,1)}, bf16[128,3072]{1,0:T(8,128)(2,1)}, bf16[128,3072]{1,0:T(8,128)(2,1)}...) custom-call(s32[1]{0:T(128)S(6)} %copy.17.length_ref, bf16[128,512]{1,0:T(8,128)(2,1)} %bitcast.16, f32[1,4096]{1,0:T(1,128)} %bitcast.17, ...), custom_call_target="tpu_custom_call" | custom-call | tf_op jit(solution)/shard_map/joint_attention/pallas_call | solution.py:700
  123.0 3.6 %hand_over.1 = (bf16[128,3072]{1,0:T(8,128)(2,1)}, bf16[128,3072]{1,0:T(8,128)(2,1)}, bf16[128,3072]{1,0:T(8,128)(2,1)}, bf16[128,3072]{1,0:T(8,128)(2,1)}, f32[128,384]{1,0:T(8,128)}, /*index=5*/f32[128,384]{1,0:T(8,128)}) custom-call(bf16[128,3072]{1,0:T(8,128)(2,1)} %get-tuple-element.18.refs_0_, bf16[128,3072]{1,0:T(8,128)(2,1)} %get-tuple-element.19.refs_1_, ...), custom_call_target="tpu_custom_call" | custom-call | tf_op jit(solution)/shard_map/hand_over/pallas_call | solution.py:723
